TPU v7x, 32 devices: a whole 2x2x4 slice. The times are simulated.
32 devices in a mesh: groups: 2 (over x), outd: 8 (over z, y), ind: 2 (over core).
Axes of the slice: x: 2, y: 2, z: 4, core: 2. Of those that a mesh axis runs over, the one named last changes fastest.
Arguments:
- activations: bfloat16 [1024, 5120], P(('groups', 'outd'), 'ind'), parts along dimension 0, may hold values from -6 to 6
- out_grads: bfloat16 [1024, 27648], P(('groups', 'ind'), 'outd'), parts along dimension 0, may hold values from -6 to 6
- query_grads: bfloat16 [4, 5120, 27648], P(None, 'ind', 'outd'), may hold values from -0.0014953613 to 0.0014953613
Outputs:
- scores: float32 [4, 1024], P(None, ('groups', 'outd', 'ind')), parts along dimension 1
There are 2 independent parts, one for each index of `groups`. A program takes and returns all parts, laid end to end along the dimension named above; an argument that names none is the same for every part. Nothing has to cross between parts.
All inputs are finite; a program needn't handle non-finite values.
Results may differ from a plain program's by a relative error of at most 0.0003.
Values may be sent and summed in bfloat16 or wider, within the bound.
A program may use at most 192 MiB of HBM per device.

v0:
```python
import jax
import jax.numpy as jnp
from jax import lax
from jax.sharding import PartitionSpec as P


def score_rows(act_block, grad_block, query_grads):
    projected = jnp.einsum(
        "ti,qio->qto", act_block, query_grads, preferred_element_type=jnp.float32
    )
    return jnp.einsum("qto,to->qt", projected, grad_block.astype(jnp.float32))


def local(activations, out_grads, query_grads):
    gradient = lax.all_gather(out_grads, "ind", axis=0, tiled=True)
    gathered = lax.all_gather(activations, "outd", axis=0, tiled=True)
    partial_sum = score_rows(gathered, gradient, query_grads)
    summed = lax.psum(partial_sum, ("outd", "ind"))
    share_len = summed.shape[1] // lax.axis_size(("outd", "ind"))
    position = lax.axis_index(("outd", "ind"))
    return lax.dynamic_slice_in_dim(summed, position * share_len, share_len, 1)


def solution(mesh):
    in_specs = (P(("groups", "outd"), "ind"), P(("groups", "ind"), "outd"), P(None, "ind", "outd"))
    out_specs = P(None, ("groups", "outd", "ind"))
    return jax.shard_map(local, mesh=mesh, in_specs=in_specs, out_specs=out_specs, check_vma=False)
```

profile of v0, /device:TPU:0, one launch (start us, length us, event | category | flops | bytes accessed | tf_op | source)
XLA Modules:
  0.0 165.3 jit_solution(15317672966876853480)
XLA Ops:
  6.5 0.0 all-gather.5.cloned.1.call-start
  6.5 0.7 all-gather.5.cloned.1.call-update
  7.3 0.0 all-gather.3.cloned.1.call-start
  7.3 0.7 all-gather.3.cloned.1.call-update
  8.0 16.3 %all-gather.5.cloned.1.call-done = bf16[512,3456]{1,0:T(8,128)(2,1)} async-done(((bf16[256,3456]{1,0:T(8,128)(2,1)}), bf16[512,3456]{1,0:T(8,128)(2,1)}) %all-gather.5.cloned.1.call-update) | async-done | bytes 3538960 | tf_op jit(solution)/shard_map/all_gather | solution.py:15
  24.3 5.9 %copy.10 = f32[512,3456]{0,1:T(8,128)} copy(bf16[512,3456]{1,0:T(8,128)(2,1)} %all-gather.5.cloned.1.call-done) | data formatting | bytes 10616832
  30.3 52.1 %all-gather.3.cloned.1.call-done = bf16[512,2560]{1,0:T(8,128)(2,1)} async-done(((bf16[64,2560]{1,0:T(8,128)(2,1)}), bf16[512,2560]{1,0:T(8,128)(2,1)}) %all-gather.3.cloned.1.call-update) | async-done | bytes 2621456 | tf_op jit(solution)/shard_map/all_gather | solution.py:16
  82.4 44.1 %fusion = f32[512,4]{0,1:T(4,128)S(1)} fusion(f32[512,3456]{0,1:T(8,128)} %copy.10, bf16[4,2560,3456]{2,1,0:T(8,128)(2,1)} %param.5, bf16[512,2560]{1,0:T(8,128)(2,1)} %all-gather.3.cloned.1.call-done), kind=kOutput, calls=%fused_computation.1 | convolution fusion | flops 36252942336 | bytes 80486400 | tf_op jit(solution)/shard_map/ti,qio->qto/dot_general | solution.py:8
  126.5 31.3 %psum.7 = f32[4,512]{1,0:T(4,128)S(1)} all-reduce(f32[4,512]{1,0:T(4,128)S(1)} %bitcast.11), channel_id=1, replica_groups=mesh['groups'=2,'outd'=8,'ind'=2] {'outd','ind'}, use_global_device_ids=true, to_apply=%region_0.0 | all-reduce | flops 2048 | bytes 16384 | tf_op jit(solution)/shard_map/psum | solution.py:18
  157.8 0.7 constant_dynamic-slice_fusion
Async XLA Ops:
  6.5 17.8 %all-gather.5.cloned.1.call-start = ((), (), s32[]{:S(2)}) async-start(), calls=%async_computation.1 | async-start | bytes 5308416 | tf_op jit(solution)/shard_map/all_gather | solution.py:15
  7.3 75.1 %all-gather.3.cloned.1.call-start = ((), (), s32[]{:S(2)}) async-start(), calls=%async_computation | async-start | bytes 2949120 | tf_op jit(solution)/shard_map/all_gather | solution.py:16
Sparse Core Ops, SparseCore 0:
  8.9 15.3 all-gather.4
  26.5 55.8 all-gather.2
where the time goes:
time: 166 us; the launch traced here: 165 us
  waiting for transfers between devices  69.8 us (42%)
  matrix products  44.1 us (27%)
  blocking collectives  31.3 us (19%)
  between operations  13.4 us (8%)
  local copies, waits for them, and re-layouts  6.6 us (4%)
    all_gather x1, waiting for transfers between devices, local(): gathered = lax.all_gather(activations, 'outd', axis=0, tiled=True)  52.1 us
    dot_general x1, matrix products, score_rows(): jnp.einsum('ti,qio->qto', act_block, query_grads, preferred_element_type=...  44.1 us
    psum x1, blocking collectives, local(): summed = lax.psum(partial_sum, ('outd', 'ind'))  31.3 us
    all_gather x1, waiting for transfers between devices, local(): gradient = lax.all_gather(out_grads, 'ind', axis=0, tiled=True)  16.3 us
    unnamed x1, local copies, waits for them, and re-layouts  5.95 us
  transfers between devices with their start and end apart: 2, of which 2 were waited for; matrix products, arithmetic and copies ran while one was open for 4% of the time, Pallas kernels for 0%

commit v1 on v0

v1 whole, which is shorter than its diff:
```python
import functools

import jax
import jax.numpy as jnp
from jax import lax
from jax.experimental import pallas as pl
from jax.experimental.pallas import tpu as pltpu
from jax.sharding import PartitionSpec as P

MESH = pl.DeviceIdType.MESH
ROWS = 256
PLANE = 2


def kernel(n_out, n_in, a_hbm, g_hbm, q_hbm, out_ref,
           a_all, g_all, w_buf, held, acc, part, inbox,
           w_sem, own_sem, g_sem, a_send, a_recv, s_send, s_recv):
    queries, width, cols = q_hbm.shape
    block_t = a_hbm.shape[0]
    half_t = g_hbm.shape[0]
    tokens = block_t * n_out
    steps = width // ROWS
    line_len = n_out // PLANE
    total = n_out * n_in
    mo, mi = lax.axis_index("outd"), lax.axis_index("ind")
    line, plane = mo // PLANE, mo % PLANE
    me = mo * n_in + mi

    def fetch(s, slot):
        return pltpu.make_async_copy(
            q_hbm.at[:, pl.ds(s * ROWS, ROWS), :], w_buf.at[slot], w_sem.at[slot])

    own_g = pltpu.make_async_copy(g_hbm, g_all.at[mi], own_sem.at[0])
    own_a = pltpu.make_async_copy(a_hbm, a_all.at[mo], own_sem.at[1])
    own_g.start()
    fetch(0, 0).start()
    own_a.start()

    barrier = pltpu.get_barrier_semaphore()
    for k in range(1, total):
        peer = lax.rem(me + k, total)
        pl.semaphore_signal(barrier, inc=1, device_id={"outd": peer // n_in, "ind": peer % n_in},
                            device_id_type=MESH)
    pl.semaphore_wait(barrier, total - 1)

    g_copy = pltpu.make_async_remote_copy(
        src_ref=g_hbm, dst_ref=g_all.at[mi], send_sem=g_sem.at[0], recv_sem=g_sem.at[1],
        device_id={"ind": 1 - mi}, device_id_type=MESH)
    g_wait = pltpu.make_async_remote_copy(
        src_ref=g_hbm, dst_ref=g_all.at[1 - mi], send_sem=g_sem.at[0], recv_sem=g_sem.at[1],
        device_id={"ind": 1 - mi}, device_id_type=MESH)
    g_copy.start()

    def hop(slot, direction, src=None):
        to = (mo + PLANE, mo - PLANE, line * PLANE + (1 - plane))[direction]
        return pltpu.make_async_remote_copy(
            src_ref=a_all.at[slot] if src is None else src, dst_ref=a_all.at[slot],
            send_sem=a_send.at[direction, slot], recv_sem=a_recv.at[slot],
            device_id={"outd": to}, device_id_type=MESH)

    hop(mo, 2, a_hbm).start()

    @pl.when(line < line_len - 1)
    def _():
        hop(mo, 0, a_hbm).start()

    @pl.when(line > 0)
    def _():
        hop(mo, 1, a_hbm).start()

    def relay(distance):
        low, high = mo - distance * PLANE, mo + distance * PLANE

        @pl.when(line >= distance)
        def _():
            hop(low, 0).wait_recv()

            @pl.when(line < line_len - 1)
            def _():
                hop(low, 0).start()

            hop(low, 2).start()

        @pl.when(line + distance < line_len)
        def _():
            hop(high, 1).wait_recv()

            @pl.when(line > 0)
            def _():
                hop(high, 1).start()

            hop(high, 2).start()

    def dot(w, g):
        return lax.dot_general(w.reshape(queries * ROWS, cols), g, (((1,), (1,)), ((), ())),
                               preferred_element_type=jnp.float32)

    def half(slot, which):
        at = pl.multiple_of(which * half_t, 128)
        held[0, :, pl.ds(at, half_t)] = dot(w_buf[slot], g_all[which])

    fetch(1, 1).start()
    own_g.wait()
    fetch(0, 0).wait()
    half(0, mi)
    g_wait.wait_recv()
    half(0, 1 - mi)

    tail = 2
    waits = {2: 1, 4: 2, 6: 3}

    def step(s, carry):
        slot = lax.rem(s, 2)
        for at, distance in waits.items():
            if distance < line_len:
                @pl.when(s == at)
                def _():
                    relay(distance)
        fetch(s + 1, 1 - slot).start()
        fetch(s, slot).wait()
        held[s] = dot(w_buf[slot], g_all[...].reshape(tokens, cols))
        return carry

    lax.fori_loop(1, steps - tail, step, 0)

    for other in range(line_len):
        hop(other * PLANE + (1 - plane), 2).wait_recv()
    own_a.wait()

    def weigh(s, block):
        a_t = a_all[:, :, s * ROWS:(s + 1) * ROWS].reshape(tokens, ROWS).astype(jnp.float32).T
        return (block.reshape(queries, ROWS // 8, 8, tokens) * a_t.reshape(ROWS // 8, 8, tokens)).sum(1)

    acc[...] = jnp.zeros_like(acc)
    done = 0
    for s in range(steps - tail, steps):
        slot = s % 2
        if s + 1 < steps:
            fetch(s + 1, 1 - slot).start()
        fetch(s, slot).wait()
        upto = s * (s - steps + tail + 1) // tail
        found = acc[...]
        for earlier in range(done, upto):
            found += weigh(earlier, held[earlier])
        done = upto
        held[s] = dot(w_buf[slot], g_all[...].reshape(tokens, cols))
        acc[...] = found
    found = acc[...]
    for earlier in range(done, steps):
        found += weigh(earlier, held[earlier])
    mine = found.sum(1)

    lanes = 128
    share = tokens // total
    per = lanes // share
    for z in range(tokens // lanes):
        part[z, 0:queries] = mine[:, z * lanes:(z + 1) * lanes]
        part[z, queries:8] = jnp.zeros((8 - queries, lanes), jnp.float32)

    def give(k):
        peer = lax.rem(me + k, total)
        return pltpu.make_async_remote_copy(
            src_ref=part.at[peer // per], dst_ref=inbox.at[k], send_sem=s_send.at[k], recv_sem=s_recv.at[k],
            device_id={"outd": peer // n_in, "ind": peer % n_in}, device_id_type=MESH)

    for k in range(1, total):
        give(k).start()

    g_copy.wait_send()
    hop(mo, 2, a_hbm).wait_send()
    for other in range(line_len):
        slot = other * PLANE + plane

        @pl.when(other != line)
        def _():
            hop(slot, 2).wait_send()

        @pl.when(jnp.logical_and(other <= line, line < line_len - 1))
        def _():
            hop(slot, 0).wait_send()

        @pl.when(jnp.logical_and(other >= line, line > 0))
        def _():
            hop(slot, 1).wait_send()

    sums = part[me // per]
    for k in range(1, total):
        give(k).wait_recv()
        sums += inbox[k]
    sums = sums[0:queries]
    place = lax.rem(me, per)
    result = sums[:, 0:share]
    for p in range(1, per):
        result = jnp.where(place == p, sums[:, p * share:(p + 1) * share], result)
    out_ref[...] = result
    for k in range(1, total):
        give(k).wait_send()


def fused(n_out, n_in, activations, out_grads, query_grads):
    queries, width, cols = query_grads.shape
    block_t, half_t = activations.shape[0], out_grads.shape[0]
    tokens, total = block_t * n_out, n_out * n_in
    steps = width // ROWS
    anywhere = pl.BlockSpec(memory_space=pl.ANY)
    dma = pltpu.SemaphoreType.DMA
    return pl.pallas_call(
        functools.partial(kernel, n_out, n_in),
        out_shape=jax.ShapeDtypeStruct((queries, tokens // total), jnp.float32),
        in_specs=[anywhere] * 3,
        out_specs=pl.BlockSpec(memory_space=pltpu.VMEM),
        scratch_shapes=[
            pltpu.VMEM((n_out, block_t, width), jnp.bfloat16),
            pltpu.VMEM((n_in, half_t, cols), jnp.bfloat16),
            pltpu.VMEM((2, queries, ROWS, cols), jnp.bfloat16),
            pltpu.VMEM((steps, queries * ROWS, tokens), jnp.float32),
            pltpu.VMEM((queries, 8, tokens), jnp.float32),
            pltpu.VMEM((tokens // 128, 8, 128), jnp.float32),
            pltpu.VMEM((total, 8, 128), jnp.float32),
            dma((2,)),
            dma((2,)),
            dma((2,)),
            dma((3, n_out)),
            dma((n_out,)),
            dma((total,)),
            dma((total,)),
        ],
        compiler_params=pltpu.CompilerParams(
            collective_id=0, has_side_effects=True, vmem_limit_bytes=60 * 2**20),
        cost_estimate=pl.CostEstimate(
            flops=2 * queries * tokens * width * cols, bytes_accessed=2 * query_grads.size, transcendentals=0),
    )(activations, out_grads, query_grads)


def plain(activations, out_grads, query_grads):
    gradient = lax.all_gather(out_grads, "ind", axis=0, tiled=True)
    gathered = lax.all_gather(activations, "outd", axis=0, tiled=True)
    projected = jnp.einsum("ti,qio->qto", gathered, query_grads, preferred_element_type=jnp.float32)
    partial_sum = jnp.einsum("qto,to->qt", projected, gradient.astype(jnp.float32))
    return lax.psum_scatter(partial_sum, ("outd", "ind"), scatter_dimension=1, tiled=True)


def local(n_out, n_in, activations, out_grads, query_grads):
    queries, width, cols = query_grads.shape
    block_t, half_t = activations.shape[0], out_grads.shape[0]
    tokens, total = block_t * n_out, n_out * n_in
    fits = (n_in == 2 and n_out == 4 * PLANE and queries <= 8 and block_t % 16 == 0 and half_t % 128 == 0
            and cols % 128 == 0 and width % (2 * ROWS) == 0 and width // ROWS >= 8 and tokens % 128 == 0
            and 128 % (tokens // total) == 0
            and (2 * queries * ROWS * cols + tokens * (cols + width)) * 2 + queries * width * tokens * 4 < 56 * 2**20)
    if fits:
        return fused(n_out, n_in, activations, out_grads, query_grads)
    return plain(activations, out_grads, query_grads)


def solution(mesh):
    in_specs = (P(("groups", "outd"), "ind"), P(("groups", "ind"), "outd"), P(None, "ind", "outd"))
    out_specs = P(None, ("groups", "outd", "ind"))
    return jax.shard_map(functools.partial(local, mesh.shape["outd"], mesh.shape["ind"]),
                         mesh=mesh, in_specs=in_specs, out_specs=out_specs, check_vma=False)
```

time: 166 us -> 59.8 us (0.36)
  waiting for transfers between devices: 69.8 us -> 0 us
  Pallas kernels: 0 us -> 58.3 us
  matrix products: 44.1 us -> 0 us
  blocking collectives: 31.3 us -> 0 us
  between operations: 13.4 us -> 0.01 us
  local copies, waits for them, and re-layouts: 6.6 us -> 1.26 us
    all_gather x2 -> x0, waiting for transfers between devices: 68.4 us -> none  [the longest x1 52.1 us: local(): gathered = lax.all_gather(activations, 'outd', axis=0, tiled=True)]
    pallas_call x0 -> x1, Pallas kernels: none -> 58.3 us  [fused(): pl.pallas_call(functools.partial(kernel, n_out, n_in), out_shape=jax.Shap...]
    dot_general x1 -> x0, matrix products: 44.1 us -> none  [score_rows(): jnp.einsum('ti,qio->qto', act_block, query_grads, preferred_element_type=...]
    psum x1 -> x0, blocking collectives: 31.3 us -> none  [local(): summed = lax.psum(partial_sum, ('outd', 'ind'))]
    unnamed x1, local copies, waits for them, and re-layouts: 5.95 us -> 1.26 us
  transfers between devices with their start and end apart: 2 -> 0, of which waited for: 2 -> 0; matrix products, arithmetic and copies ran while one was open for 4% -> 0% of each run, Pallas kernels for 0% -> 0%
where the time goes in v1:
time: 59.8 us; the launch traced here: 59.6 us
  Pallas kernels  58.3 us (97%)
  local copies, waits for them, and re-layouts  1.26 us (2%)
    pallas_call x1, Pallas kernels, fused(): pl.pallas_call(functools.partial(kernel, n_out, n_in), out_shape=jax.Shap...  58.3 us
    unnamed x1, local copies, waits for them, and re-layouts  1.26 us

profile of v1, /device:TPU:0, one launch (start us, length us, event | category | flops | bytes accessed | tf_op | source)
XLA Modules:
  0.0 59.6 jit_solution(1182333677347801168)
XLA Ops:
  0.0 58.3 %shard_map.37 = f32[4,32]{1,0:T(4,128)} custom-call(bf16[64,2560]{1,0:T(8,128)(2,1)} %a_hbm.1, bf16[256,3456]{1,0:T(8,128)(2,1)} %g_hbm.1, bf16[4,2560,3456]{2,1,0:T(8,128)(2,1)} %q_hbm.1), custom_call_target="tpu_custom_call" | custom-call | flops 36238786560 | bytes 70778880 | tf_op jit(solution)/shard_map/pallas_call | solution.py:207
  58.3 1.3 %copy.5 = f32[4,32]{1,0:T(4,128)} copy(f32[4,32]{1,0:T(4,128)} %shard_map.37) | data formatting | bytes 1024

commit v2 on v1

--- a/solution.py
+++ b/solution.py
@@ -30,10 +30,18 @@
         return pltpu.make_async_copy(
             q_hbm.at[:, pl.ds(s * ROWS, ROWS), :], w_buf.at[slot], w_sem.at[slot])
 
+    pair = queries // 2
+
+    def first(p):
+        at = pl.ds(p * pair, pair)
+        return pltpu.make_async_copy(
+            q_hbm.at[at, pl.ds(0, ROWS), :], w_buf.at[0, at], w_sem.at[3 * p])
+
     own_g = pltpu.make_async_copy(g_hbm, g_all.at[mi], own_sem.at[0])
     own_a = pltpu.make_async_copy(a_hbm, a_all.at[mo], own_sem.at[1])
     own_g.start()
-    fetch(0, 0).start()
+    for p in range(2):
+        first(p).start()
     own_a.start()
 
     barrier = pltpu.get_barrier_semaphore()
@@ -92,36 +100,44 @@
             hop(high, 2).start()
 
     def dot(w, g):
-        return lax.dot_general(w.reshape(queries * ROWS, cols), g, (((1,), (1,)), ((), ())),
+        return lax.dot_general(w.reshape(w.shape[0] * ROWS, cols), g, (((1,), (1,)), ((), ())),
                                preferred_element_type=jnp.float32)
 
-    def half(slot, which):
+    def half(s, which):
         at = pl.multiple_of(which * half_t, 128)
-        held[0, :, pl.ds(at, half_t)] = dot(w_buf[slot], g_all[which])
-
-    fetch(1, 1).start()
+        held[s, :, pl.ds(at, half_t)] = dot(w_buf[s], g_all[which])
+
     own_g.wait()
-    fetch(0, 0).wait()
-    half(0, mi)
+    at = pl.multiple_of(mi * half_t, 128)
+    for p in range(2):
+        first(p).wait()
+        if p == 1:
+            fetch(1, 1).start()
+        held[0, p * pair * ROWS:(p + 1) * pair * ROWS, pl.ds(at, half_t)] = dot(
+            w_buf[0, p * pair:(p + 1) * pair], g_all[mi])
+    fetch(1, 1).wait()
+    fetch(2, 2).start()
+    half(1, mi)
     g_wait.wait_recv()
     half(0, 1 - mi)
+    half(1, 1 - mi)
 
     tail = 2
     waits = {2: 1, 4: 2, 6: 3}
 
     def step(s, carry):
-        slot = lax.rem(s, 2)
+        slot = lax.rem(s, 3)
         for at, distance in waits.items():
             if distance < line_len:
                 @pl.when(s == at)
                 def _():
                     relay(distance)
-        fetch(s + 1, 1 - slot).start()
+        fetch(s + 1, lax.rem(s + 1, 3)).start()
         fetch(s, slot).wait()
         held[s] = dot(w_buf[slot], g_all[...].reshape(tokens, cols))
         return carry
 
-    lax.fori_loop(1, steps - tail, step, 0)
+    lax.fori_loop(2, steps - tail, step, 0)
 
     for other in range(line_len):
         hop(other * PLANE + (1 - plane), 2).wait_recv()
@@ -134,9 +150,9 @@
     acc[...] = jnp.zeros_like(acc)
     done = 0
     for s in range(steps - tail, steps):
-        slot = s % 2
+        slot = s % 3
         if s + 1 < steps:
-            fetch(s + 1, 1 - slot).start()
+            fetch(s + 1, (s + 1) % 3).start()
         fetch(s, slot).wait()
         upto = s * (s - steps + tail + 1) // tail
         found = acc[...]
@@ -187,12 +203,7 @@
     for k in range(1, total):
         give(k).wait_recv()
         sums += inbox[k]
-    sums = sums[0:queries]
-    place = lax.rem(me, per)
-    result = sums[:, 0:share]
-    for p in range(1, per):
-        result = jnp.where(place == p, sums[:, p * share:(p + 1) * share], result)
-    out_ref[...] = result
+    out_ref[...] = sums
     for k in range(1, total):
         give(k).wait_send()
 
@@ -201,23 +212,24 @@
     queries, width, cols = query_grads.shape
     block_t, half_t = activations.shape[0], out_grads.shape[0]
     tokens, total = block_t * n_out, n_out * n_in
+    share = tokens // total
     steps = width // ROWS
     anywhere = pl.BlockSpec(memory_space=pl.ANY)
     dma = pltpu.SemaphoreType.DMA
-    return pl.pallas_call(
+    sums = pl.pallas_call(
         functools.partial(kernel, n_out, n_in),
-        out_shape=jax.ShapeDtypeStruct((queries, tokens // total), jnp.float32),
+        out_shape=jax.ShapeDtypeStruct((8, 128), jnp.float32),
         in_specs=[anywhere] * 3,
         out_specs=pl.BlockSpec(memory_space=pltpu.VMEM),
         scratch_shapes=[
             pltpu.VMEM((n_out, block_t, width), jnp.bfloat16),
             pltpu.VMEM((n_in, half_t, cols), jnp.bfloat16),
-            pltpu.VMEM((2, queries, ROWS, cols), jnp.bfloat16),
+            pltpu.VMEM((3, queries, ROWS, cols), jnp.bfloat16),
             pltpu.VMEM((steps, queries * ROWS, tokens), jnp.float32),
             pltpu.VMEM((queries, 8, tokens), jnp.float32),
             pltpu.VMEM((tokens // 128, 8, 128), jnp.float32),
             pltpu.VMEM((total, 8, 128), jnp.float32),
-            dma((2,)),
+            dma((4,)),
             dma((2,)),
             dma((2,)),
             dma((3, n_out)),
@@ -230,6 +242,8 @@
         cost_estimate=pl.CostEstimate(
             flops=2 * queries * tokens * width * cols, bytes_accessed=2 * query_grads.size, transcendentals=0),
     )(activations, out_grads, query_grads)
+    place = lax.rem(lax.axis_index(("outd", "ind")), 128 // share)
+    return lax.dynamic_slice(sums, (0, place * share), (queries, share))
 
 
 def plain(activations, out_grads, query_grads):
@@ -244,10 +258,10 @@
     queries, width, cols = query_grads.shape
     block_t, half_t = activations.shape[0], out_grads.shape[0]
     tokens, total = block_t * n_out, n_out * n_in
-    fits = (n_in == 2 and n_out == 4 * PLANE and queries <= 8 and block_t % 16 == 0 and half_t % 128 == 0
+    fits = (n_in == 2 and n_out == 4 * PLANE and queries <= 8 and queries % 2 == 0 and block_t % 16 == 0 and half_t % 128 == 0
             and cols % 128 == 0 and width % (2 * ROWS) == 0 and width // ROWS >= 8 and tokens % 128 == 0
             and 128 % (tokens // total) == 0
-            and (2 * queries * ROWS * cols + tokens * (cols + width)) * 2 + queries * width * tokens * 4 < 56 * 2**20)
+            and (3 * queries * ROWS * cols + tokens * (cols + width)) * 2 + queries * width * tokens * 4 < 56 * 2**20)
     if fits:
         return fused(n_out, n_in, activations, out_grads, query_grads)
     return plain(activations, out_grads, query_grads)

time: 59.8 us -> 58.1 us (0.972)
  Pallas kernels: 58.3 us -> 56.6 us
    pallas_call x1, Pallas kernels: 58.3 us -> 56.6 us  [fused(): pl.pallas_call(functools.partial(kernel, n_out, n_in), out_shape=jax.Shap...]
    dynamic_slice x0 -> x1, local copies, waits for them, and re-layouts: none -> 1.34 us  [fused(): return lax.dynamic_slice(sums, (0, place * share), (queries, share))]
    unnamed x1 -> x0, local copies, waits for them, and re-layouts: 1.26 us -> none
where the time goes in v2:
time: 58.1 us; the launch traced here: 58 us
  Pallas kernels  56.6 us (97%)
  local copies, waits for them, and re-layouts  1.34 us (2%)
    pallas_call x1, Pallas kernels, fused(): pl.pallas_call(functools.partial(kernel, n_out, n_in), out_shape=jax.Shap...  56.6 us
    dynamic_slice x1, local copies, waits for them, and re-layouts, fused(): return lax.dynamic_slice(sums, (0, place * share), (queries, share))  1.34 us

profile of v2, /device:TPU:0, one launch (start us, length us, event | category | flops | bytes accessed | tf_op | source)
XLA Modules:
  0.0 58.0 jit_solution(4472847115084391856)
XLA Ops:
  0.0 56.6 %shard_map.37 = f32[8,128]{1,0:T(8,128)} custom-call(bf16[64,2560]{1,0:T(8,128)(2,1)} %a_hbm.1, bf16[256,3456]{1,0:T(8,128)(2,1)} %g_hbm.1, bf16[4,2560,3456]{2,1,0:T(8,128)(2,1)} %q_hbm.1), custom_call_target="tpu_custom_call" | custom-call | flops 36238786560 | bytes 70778880 | tf_op jit(solution)/shard_map/pallas_call | solution.py:219
  56.6 1.3 %constant_dynamic-slice_fusion = f32[4,32]{1,0:T(4,128)} fusion(f32[8,128]{1,0:T(8,128)} %shard_map.37, s32[]{:T(128)S(6)} %select_n.3), kind=kLoop, calls=%fused_computation | loop fusion | bytes 1028 | tf_op jit(solution)/shard_map/dynamic_slice | solution.py:246
